TPU v7x, 256 devices: a whole 4x4x8 slice. The times are simulated.
256 devices in a mesh: col: 64 (over y, z_lo, x, core), row: 4 (over z_hi).
Axes of the slice: x: 4, y: 4, z: 8 (z_hi: 4, z_lo: 2; z = z_hi * 2 + z_lo), core: 2. Of those that a mesh axis runs over, the one named last changes fastest.
Arguments:
- root_inverse: float32 [2048, 2048], P('row', 'col')
- child_inverse: float32 [256, 512, 512], P(('col', 'row'))
- child_panel: float32 [256, 1024, 512], P(('col', 'row')), may hold values from -0.375 to 0.375
- structure: int32 [256, 8], P(('col', 'row')), may hold values from 0 to 15, as said below
- widths: int32 [256], P(('col', 'row')), may hold values from 256 to 512
Outputs:
- sigma_root: float32 [2048, 2048], P('row', 'col')
- child_cross: float32 [256, 1024, 512], P(('col', 'row'))
- child_variance: float32 [256, 512], P(('col', 'row'))
Inputs may be any that keep to these rules, and one draw needn't show every extreme that they name: `structure`: each child names 8 distinct root blocks in rising order.
All inputs are finite; a program needn't handle non-finite values.
Results may differ from a plain program's by a relative error of at most 0.0003.
Values sent between devices are 32-bit elements; how exact they have to be, the bound alone decides.
No kernel may reach another device: no remote copies, remote signals or barrier semaphores. Data moves between devices by JAX's collectives and lax.ppermute only.
A program may use at most 192 MiB of HBM per device.

v0:
```python
import jax
import jax.numpy as jnp
from jax import lax
from jax.sharding import PartitionSpec as P

TILE = 128


def body(root_inverse, child_inverse, child_panel, structure, widths):
    partial_value = jnp.dot(
        lax.all_gather(root_inverse, "col", axis=1, tiled=True).T,
        root_inverse,
        precision=lax.Precision.HIGHEST,
        preferred_element_type=jnp.float32,
    )
    own_block = lax.psum_scatter(partial_value, "row", scatter_dimension=0, tiled=True)
    wide_rows = lax.all_gather(own_block, "col", axis=1, tiled=True)
    complete = lax.all_gather(wide_rows, "row", axis=0, tiled=True)
    tile_count = complete.shape[0] // TILE
    tiled = complete.reshape(tile_count, TILE, tile_count, TILE)

    def handle(items):
        inverse_block, panel_block, tiles, width_value = items
        column_ids = jnp.arange(inverse_block.shape[0], dtype=jnp.int32)
        live_cols = (column_ids < width_value).astype(jnp.float32)
        masked_inverse = inverse_block * live_cols[:, None] * live_cols[None, :]
        masked_panel = panel_block * live_cols[None, :]
        update = jnp.dot(
            masked_panel,
            masked_inverse,
            precision=lax.Precision.HIGHEST,
            preferred_element_type=jnp.float32,
        )
        picked = jnp.take(jnp.take(tiled, tiles, axis=0), tiles, axis=2)
        ancestor_block = picked.reshape(tiles.shape[0] * TILE, tiles.shape[0] * TILE)
        cross_block = -jnp.dot(
            ancestor_block,
            update,
            precision=lax.Precision.HIGHEST,
            preferred_element_type=jnp.float32,
        )
        variance = jnp.sum(masked_inverse * masked_inverse, axis=0) - jnp.sum(
            update * cross_block, axis=0
        )
        return (cross_block, variance)

    child_cross, child_variance = lax.map(handle, (child_inverse, child_panel, structure, widths))
    return (own_block, child_cross, child_variance)


def solution(mesh):
    placed = (
        P("row", "col"),
        P(("col", "row"), None, None),
        P(("col", "row"), None, None),
        P(("col", "row"), None),
        P(("col", "row")),
    )
    return jax.shard_map(
        body,
        mesh=mesh,
        in_specs=placed,
        out_specs=(P("row", "col"), P(("col", "row"), None, None), P(("col", "row"), None)),
        check_vma=False,
    )
```

profile of v0, /device:TPU:1, one launch (start us, length us, event | category | flops | bytes accessed | tf_op | source)
XLA Modules:
  0.0 641.0 jit_solution(5670676339828152946)
XLA Ops:
  7.2 0.0 all-gather.4.cloned.1.call-start
  7.2 0.7 all-gather.4.cloned.1.call-update
  7.9 0.0 copy-start.1
  7.9 0.0 copy-start
  7.9 0.0 reduce-scatter.2.cloned.1.call-start
  8.0 114.6 %all-gather.4.cloned.1.call-done = f32[512,2048]{0,1:T(8,128)} async-done(((f32[512,32]{0,1:T(8,128)}), f32[512,2048]{0,1:T(8,128)}) %all-gather.4.cloned.1.call-update) | async-done | bytes 4194320 | tf_op jit(solution)/shard_map/all_gather | solution.py:11
  122.5 6.8 %fusion.19 = f32[2048,32]{0,1:T(8,128)} fusion(f32[512,2048]{0,1:T(8,128)} %all-gather.4.cloned.1.call-done, f32[512,32]{0,1:T(8,128)} %param.5), kind=kOutput, calls=%fused_computation.32 | convolution fusion | flops 402653184 | bytes 4521984 | tf_op jit(solution)/shard_map/dot_general | solution.py:10
  129.3 0.0 reduce-scatter.2.cloned.1.call-update
  129.3 0.0 all-gather.6.cloned.1.call-start
  129.4 21.8 %reduce-scatter.2.cloned.1.call-done = f32[512,32]{0,1:T(8,128)} async-done(((f32[2048,32]{0,1:T(8,128)}), f32[512,32]{0,1:T(8,128)}) %reduce-scatter.2.cloned.1.call-update) | async-done | bytes 65552 | tf_op jit(solution)/shard_map/reduce_scatter | solution.py:16
  151.2 0.0 all-gather.6.cloned.1.call-update
  151.2 0.0 all-gather.8.cloned.1.call-start
  151.3 112.2 %all-gather.6.cloned.1.call-done = f32[512,2048]{0,1:T(8,128)} async-done(((f32[512,32]{0,1:T(8,128)}), f32[512,2048]{0,1:T(8,128)}) %all-gather.6.cloned.1.call-update) | async-done | bytes 4194320 | tf_op jit(solution)/shard_map/all_gather | solution.py:17
  263.5 0.0 all-gather.8.cloned.1.call-update
  264.2 0.0 copy-done.1
  264.2 0.0 copy-done
  264.2 0.2 fusion.9
  264.4 0.1 broadcast_bitcast_fusion
  264.5 5.2 fusion.2
  269.7 289.6 %all-gather.8.cloned.1.call-done = f32[2048,2048]{0,1:T(8,128)} async-done(((f32[512,2048]{0,1:T(8,128)}), f32[2048,2048]{0,1:T(8,128)}) %all-gather.8.cloned.1.call-update) | async-done | bytes 16777232 | tf_op jit(solution)/shard_map/all_gather | solution.py:18
  559.3 14.1 %copy.14 = f32[256,8,16,128]{3,2,1,0:T(8,128)} copy(f32[256,8,16,128]{3,1,2,0:T(8,128)} %bitcast.45) | data formatting | bytes 33554432
  573.4 21.5 %copy.11 = f32[16,128,16,128]{3,2,1,0:T(8,128)} copy(f32[16,128,16,128]{1,0,3,2:T(8,128)} %bitcast.43) | data formatting | bytes 33554432 | tf_op jit(solution)/shard_map/reshape | solution.py:20
  594.8 10.1 %gather_fusion = f32[8,128,16,128]{3,2,1,0:T(8,128)} fusion(f32[16,128,16,128]{3,2,1,0:T(8,128)} %copy.11, s32[1024]{0:T(1024)S(1)} %pad_clamp_fusion), kind=kCustom, calls=%fused_computation | custom fusion | bytes 16777248 | tf_op jit(solution)/shard_map/while/body/eval_jaxpr/jit(_take)/gather | solution.py:34
  604.9 4.2 broadcast_select_fusion
  609.1 5.7 copy.12
  614.8 6.2 gather_fusion.1
  621.0 4.6 copy.13
  625.5 8.3 %multiply_reduce_fusion = (f32[512]{0:T(512)S(1)}, f32[1,1024,512]{2,1,0:T(8,128)}) fusion(f32[1024,512]{1,0:T(8,128)S(1)} %fusion.2, f32[128,8,8,128]{3,2,1,0:T(8,128)S(1)} %bitcast.44, pred[1024]{0:T(1024)(128)(4,1)S(1)} %broadcast_bitcast_fusion), kind=kOutput, calls=%fused_computation.8 | convolution fusion | flops 6445071872 | bytes 8391680 | tf_op jit(solution)/shard_map/while/body/eval_jaxpr/dot_general | solution.py:36
  633.9 0.6 sub.14
  (4 shorter events, 0.0 us)
Async XLA Ops:
  7.2 115.4 %all-gather.4.cloned.1.call-start = ((), (), s32[]{:S(2)}) async-start(), calls=%async_computation.1 | async-start | bytes 4259840 | tf_op jit(solution)/shard_map/all_gather | solution.py:11
  7.9 256.3 %copy-start.1 = (s32[1,8]{1,0:T(1,128)S(1)}, s32[1,8]{1,0:T(1,128)}, u32[]{:S(2)}) copy-start(s32[1,8]{1,0:T(1,128)} %param.8) | copy-start | bytes 100
  7.9 256.3 %copy-start = (f32[1,512,512]{2,1,0:T(8,128)S(1)}, f32[1,512,512]{2,1,0:T(8,128)}, u32[]{:S(2)}) copy-start(f32[1,512,512]{2,1,0:T(8,128)} %param.6) | copy-start | bytes 3145732
  7.9 143.3 %reduce-scatter.2.cloned.1.call-start = ((), (), s32[]{:S(2)}) async-start(), calls=%async_computation.2 | async-start | bytes 327680 | tf_op jit(solution)/shard_map/reduce_scatter | solution.py:16
  129.3 134.1 %all-gather.6.cloned.1.call-start = ((), (), s32[]{:S(2)}) async-start(), calls=%async_computation.3 | async-start | bytes 4259840 | tf_op jit(solution)/shard_map/all_gather | solution.py:17
  151.2 408.0 %all-gather.8.cloned.1.call-start = ((), (), s32[]{:S(2)}) async-start(), calls=%async_computation.4 | async-start | bytes 20971520 | tf_op jit(solution)/shard_map/all_gather | solution.py:18
Sparse Core Ops, SparseCore 0:
  9.9 112.6 all-gather.3
  129.5 21.7 reduce-scatter.1
  153.8 109.6 all-gather.5
  265.3 293.9 all-gather.7
where the time goes:
time: 641 us
  waiting for transfers between devices  539 us (84%)
  local copies, waits for them, and re-layouts  62.2 us (10%)
  matrix products  20.3 us (3%)
  between operations  14.5 us (2%)
    all_gather x1, waiting for transfers between devices, body(): complete = lax.all_gather(wide_rows, 'row', axis=0, tiled=True)  290 us
    all_gather x1, waiting for transfers between devices, body(): lax.all_gather(root_inverse, 'col', axis=1, tiled=True)  115 us
    all_gather x1, waiting for transfers between devices, body(): wide_rows = lax.all_gather(own_block, 'col', axis=1, tiled=True)  112 us
    reduce_scatter x1, waiting for transfers between devices, body(): lax.psum_scatter(partial_value, 'row', scatter_dimension=0, tiled=True)  21.8 us
    reshape x1, local copies, waits for them, and re-layouts, body(): tiled = complete.reshape(tile_count, TILE, tile_count, TILE)  21.5 us
    gather x3, local copies, waits for them, and re-layouts, handle(): picked = jnp.take(jnp.take(tiled, tiles, axis=0), tiles, axis=2)  20.8 us
    unnamed x5, local copies, waits for them, and re-layouts  14.1 us
  transfers between devices with their start and end apart: 4, of which 4 were waited for; matrix products, arithmetic and copies ran while one was open for 1% of the time, Pallas kernels for 0%

commit v1 on v0

--- a/solution.py
+++ b/solution.py
@@ -15,7 +15,9 @@
     )
     own_block = lax.psum_scatter(partial_value, "row", scatter_dimension=0, tiled=True)
     wide_rows = lax.all_gather(own_block, "col", axis=1, tiled=True)
-    complete = lax.all_gather(wide_rows, "row", axis=0, tiled=True)
+    complete = jnp.concatenate(
+        lax.all_to_all(jnp.stack([wide_rows] * lax.axis_size("row")), "row", 0, 0), axis=0
+    )
     tile_count = complete.shape[0] // TILE
     tiled = complete.reshape(tile_count, TILE, tile_count, TILE)
 

time: 641 us -> 714 us (1.11)
  waiting for transfers between devices: 539 us -> 610 us
    all_to_all x0 -> x1, waiting for transfers between devices: none -> 361 us  [body(): lax.all_to_all(jnp.stack([wide_rows] * lax.axis_size('row')), 'row', 0, 0)]
    all_gather x1 -> x0, waiting for transfers between devices: 290 us -> none  [body(): complete = lax.all_gather(wide_rows, 'row', axis=0, tiled=True)]
    reshape x1 -> x0, local copies, waits for them, and re-layouts: 21.5 us -> none  [body(): tiled = complete.reshape(tile_count, TILE, tile_count, TILE)]
    another operation x0 -> x1, local copies, waits for them, and re-layouts: none -> 10.1 us  [body(): jnp.stack([wide_rows] * lax.axis_size('row'))]
where the time goes in v1:
time: 714 us; the launch traced here: 713 us
  waiting for transfers between devices  610 us (85%)
  local copies, waits for them, and re-layouts  56.2 us (8%)
  matrix products  20.3 us (3%)
  between operations  14.5 us (2%)
  starting transfers between devices  7.21 us (1%)
    all_to_all x1, waiting for transfers between devices, body(): lax.all_to_all(jnp.stack([wide_rows] * lax.axis_size('row')), 'row', 0, 0)  361 us
    all_gather x1, waiting for transfers between devices, body(): lax.all_gather(root_inverse, 'col', axis=1, tiled=True)  115 us
    all_gather x1, waiting for transfers between devices, body(): wide_rows = lax.all_gather(own_block, 'col', axis=1, tiled=True)  112 us
    reduce_scatter x1, waiting for transfers between devices, body(): lax.psum_scatter(partial_value, 'row', scatter_dimension=0, tiled=True)  21.9 us
    gather x3, local copies, waits for them, and re-layouts, handle(): picked = jnp.take(jnp.take(tiled, tiles, axis=0), tiles, axis=2)  20.8 us
  transfers between devices with their start and end apart: 4, of which 4 were waited for; matrix products, arithmetic and copies ran while one was open for 1% of the time, Pallas kernels for 0%

profile of v1, /device:TPU:1, one launch (start us, length us, event | category | flops | bytes accessed | tf_op | source)
XLA Modules:
  0.0 713.3 jit_solution(10571682048371239800)
XLA Ops:
  7.2 0.0 all-gather.3.cloned.1.call-start
  7.2 0.7 all-gather.3.cloned.1.call-update
  7.9 0.0 reduce-scatter.2.cloned.1.call-start
  7.9 114.6 %all-gather.3.cloned.1.call-done = f32[512,2048]{0,1:T(8,128)} async-done(((f32[512,32]{0,1:T(8,128)}), f32[512,2048]{0,1:T(8,128)}) %all-gather.3.cloned.1.call-update) | async-done | bytes 4194320 | tf_op jit(solution)/shard_map/all_gather | solution.py:11
  122.5 6.8 fusion.19
  129.3 0.0 reduce-scatter.2.cloned.1.call-update
  129.3 0.0 all-gather.5.cloned.1.call-start
  129.4 21.9 %reduce-scatter.2.cloned.1.call-done = f32[512,32]{0,1:T(8,128)} async-done(((f32[2048,32]{0,1:T(8,128)}), f32[512,32]{0,1:T(8,128)}) %reduce-scatter.2.cloned.1.call-update) | async-done | bytes 65552 | tf_op jit(solution)/shard_map/reduce_scatter | solution.py:16
  151.2 0.0 all-gather.5.cloned.1.call-update
  151.3 112.2 %all-gather.5.cloned.1.call-done = f32[512,2048]{0,1:T(8,128)} async-done(((f32[512,32]{0,1:T(8,128)}), f32[512,2048]{0,1:T(8,128)}) %all-gather.5.cloned.1.call-update) | async-done | bytes 4194320 | tf_op jit(solution)/shard_map/all_gather | solution.py:17
  263.5 5.5 copy.10
  269.0 10.1 %stack.2 = f32[4,512,2048]{2,1,0:T(8,128)} broadcast(f32[512,2048]{1,0:T(8,128)} %copy.10), dimensions={1,2} | broadcast | bytes 20971520 | tf_op jit(solution)/shard_map/stack | solution.py:19
  279.0 0.0 copy-start.1
  279.0 0.0 copy-start
  279.0 7.1 all-to-all-start
  286.8 0.0 copy-done.1
  286.8 0.0 copy-done
  286.8 0.2 fusion.9
  287.1 0.1 broadcast_bitcast_fusion
  287.1 5.2 fusion.2
  292.3 360.7 %all-to-all-done = f32[4,512,2048]{2,1,0:T(8,128)} async-done(((f32[4,512,2048]{2,1,0:T(8,128)}), f32[4,512,2048]{2,1,0:T(8,128)}, u32[]{:S(2)}, u32[]{:S(2)}) %all-to-all-start) | async-done | bytes 16777248 | tf_op jit(solution)/shard_map/all_to_all | solution.py:19
  653.1 14.1 %copy.13 = f32[256,8,16,128]{3,2,1,0:T(8,128)} copy(f32[256,8,16,128]{3,1,2,0:T(8,128)} %bitcast.12) | data formatting | bytes 33554432
  667.1 10.1 %gather_fusion = f32[8,128,16,128]{3,2,1,0:T(8,128)} fusion(f32[16,128,16,128]{3,2,1,0:T(8,128)} %bitcast.42, s32[1024]{0:T(1024)S(1)} %pad_clamp_fusion), kind=kCustom, calls=%fused_computation | custom fusion | bytes 16777248 | tf_op jit(solution)/shard_map/while/body/eval_jaxpr/jit(_take)/gather | solution.py:36
  677.2 4.2 broadcast_select_fusion
  681.4 5.7 copy.11
  687.1 6.1 gather_fusion.1
  693.3 4.6 copy.12
  697.8 8.3 %multiply_reduce_fusion = (f32[512]{0:T(512)S(1)}, f32[1,1024,512]{2,1,0:T(8,128)}) fusion(f32[1024,512]{1,0:T(8,128)S(1)} %fusion.2, f32[128,8,8,128]{3,2,1,0:T(8,128)S(1)} %bitcast.43, pred[1024]{0:T(1024)(128)(4,1)S(1)} %broadcast_bitcast_fusion), kind=kOutput, calls=%fused_computation.8 | convolution fusion | flops 6445071872 | bytes 8391680 | tf_op jit(solution)/shard_map/while/body/eval_jaxpr/dot_general | solution.py:38
  706.2 0.6 sub.14
  (4 shorter events, 0.0 us)
Async XLA Ops:
  7.2 115.4 %all-gather.3.cloned.1.call-start = ((), (), s32[]{:S(2)}) async-start(), calls=%async_computation.2 | async-start | bytes 4259840 | tf_op jit(solution)/shard_map/all_gather | solution.py:11
  7.9 143.3 %reduce-scatter.2.cloned.1.call-start = ((), (), s32[]{:S(2)}) async-start(), calls=%async_computation.3 | async-start | bytes 327680 | tf_op jit(solution)/shard_map/reduce_scatter | solution.py:16
  129.3 134.1 %all-gather.5.cloned.1.call-start = ((), (), s32[]{:S(2)}) async-start(), calls=%async_computation.4 | async-start | bytes 4259840 | tf_op jit(solution)/shard_map/all_gather | solution.py:17
  279.0 7.8 %copy-start.1 = (s32[1,8]{1,0:T(1,128)S(1)}, s32[1,8]{1,0:T(1,128)}, u32[]{:S(2)}) copy-start(s32[1,8]{1,0:T(1,128)} %param.8) | copy-start | bytes 100
  279.0 7.8 %copy-start = (f32[1,512,512]{2,1,0:T(8,128)S(1)}, f32[1,512,512]{2,1,0:T(8,128)}, u32[]{:S(2)}) copy-start(f32[1,512,512]{2,1,0:T(8,128)} %param.6) | copy-start | bytes 3145732
  279.0 374.0 %all-to-all-start = ((f32[4,512,2048]{2,1,0:T(8,128)}), f32[4,512,2048]{2,1,0:T(8,128)}, u32[]{:S(2)}, u32[]{:S(2)}) async-start(f32[4,512,2048]{2,1,0:T(8,128)} %stack.2), calls=%async_computation.1 | async-start | bytes 33554432 | tf_op jit(solution)/shard_map/all_to_all | solution.py:19
Sparse Core Ops, SparseCore 0:
  9.9 112.6 all-gather.2
  129.5 21.7 reduce-scatter.1
  153.8 109.6 all-gather.4
